TPU v7x, 32 devices: a whole 2x2x4 slice. The times are simulated.
32 devices in a mesh: groups: 2 (over x), gx: 8 (over z, y), gy: 2 (over core).
Axes of the slice: x: 2, y: 2, z: 4, core: 2. Of those that a mesh axis runs over, the one named last changes fastest.
Arguments:
- state: float32 [10, 32, 16, 128], P('groups', 'gx', 'gy'), parts along dimension 0, may hold values from -1.5 to 7, as said below
- closure: float32 [64, 16, 128], P(('groups', 'gx'), 'gy'), parts along dimension 0, may hold values from 0.05 to 0.4
- cotangent: float32 [10, 32, 16, 128], P('groups', 'gx', 'gy'), parts along dimension 0, may hold values from -6 to 6
Outputs:
- grad_state: float32 [10, 32, 16, 128], P('groups', 'gx', 'gy'), parts along dimension 0
- grad_closure: float32 [64, 16, 128], P(('groups', 'gx'), 'gy'), parts along dimension 0
There are 2 independent parts, one for each index of `groups`. A program takes and returns all parts, laid end to end along the dimension named above; each array names one. Nothing has to cross between parts.
Inputs may be any that keep to these rules, and one draw needn't show every extreme that they name: Each cell holds a gas state: rho in 0.5 to 2, pressure 0.4 (E - |m|^2 / (2 rho)) in 0.5 to 2, each velocity component m_d / rho within -0.75 to 0.75.
All inputs are finite; a program needn't handle non-finite values.
Results may differ from a plain program's by a relative error of at most 0.00006.
Values sent between devices are 32-bit elements; how exact they have to be, the bound alone decides.
A program may use at most 128 MiB of HBM per device.

v0:
```python
import jax
import jax.numpy as jnp
from jax import lax
from jax.sharding import PartitionSpec as P

WENO_EPS = 1e-06
TIME_STEP = 0.06
SECTION_WEIGHTS = ((0.0, 1.0), (0.75, 0.25), (1.0 / 3.0, 2.0 / 3.0))


def with_halo(cells, sides, width):
    for axis, dim in sides:
        count = lax.axis_size(axis)
        head = lax.slice_in_dim(cells, 0, width, axis=dim)
        tail = lax.slice_in_dim(cells, cells.shape[dim] - width, cells.shape[dim], axis=dim)
        cells = jnp.concatenate(
            [
                lax.ppermute(tail, axis, [(i, (i + 1) % count) for i in range(count)]),
                cells,
                lax.ppermute(head, axis, [((i + 1) % count, i) for i in range(count)]),
            ],
            axis=dim,
        )
    return cells


def passed_along(value, axis, steps):
    count = lax.axis_size(axis)
    pairs = [(source, (source + steps) % count) for source in range(count)]
    return lax.ppermute(value, axis, pairs)


def window(block, start, extent, along):
    return lax.slice_in_dim(block, start, start + extent, axis=along)


def split_fluxes(fields, direction):
    density = fields[0]
    energy = fields[4]
    inverse = 1.0 / density
    kinetic = (
        0.5 * (fields[1] * fields[1] + fields[2] * fields[2] + fields[3] * fields[3]) * inverse
    )
    pressure = 0.4 * (energy - kinetic)
    speed = fields[1 + direction] * inverse
    wave_speed = 1.5 * jnp.sqrt(speed * speed + 1.4 * pressure * inverse)
    fluxes = [
        fields[1 + direction],
        fields[1] * speed,
        fields[2] * speed,
        fields[3] * speed,
        (energy + pressure) * speed,
    ]
    fluxes[1 + direction] = fluxes[1 + direction] + pressure
    fluxes = jnp.stack(fluxes)
    upwind = 0.5 * (fluxes + wave_speed * fields)
    downwind = 0.5 * (fluxes - wave_speed * fields)
    return (upwind, downwind)


def weno_face(left_two, left_one, centre, right_one, right_two):
    cand_zero = (2.0 * left_two - 7.0 * left_one + 11.0 * centre) / 6.0
    cand_one = (-left_one + 5.0 * centre + 2.0 * right_one) / 6.0
    cand_two = (2.0 * centre + 5.0 * right_one - right_two) / 6.0
    rough_zero = (
        13.0 / 12.0 * (left_two - 2.0 * left_one + centre) ** 2
        + 0.25 * (left_two - 4.0 * left_one + 3.0 * centre) ** 2
    )
    rough_one = (
        13.0 / 12.0 * (left_one - 2.0 * centre + right_one) ** 2
        + 0.25 * (left_one - right_one) ** 2
    )
    rough_two = (
        13.0 / 12.0 * (centre - 2.0 * right_one + right_two) ** 2
        + 0.25 * (3.0 * centre - 4.0 * right_one + right_two) ** 2
    )
    weight_zero = 0.1 / (WENO_EPS + rough_zero) ** 2
    weight_one = 0.6 / (WENO_EPS + rough_one) ** 2
    weight_two = 0.3 / (WENO_EPS + rough_two) ** 2
    return (weight_zero * cand_zero + weight_one * cand_one + weight_two * cand_two) / (
        weight_zero + weight_one + weight_two
    )


def axis_rate(upwind, downwind, along, extent):
    faces = extent + 1
    upper = weno_face(
        window(upwind, 0, faces, along),
        window(upwind, 1, faces, along),
        window(upwind, 2, faces, along),
        window(upwind, 3, faces, along),
        window(upwind, 4, faces, along),
    )
    lower = weno_face(
        window(downwind, 5, faces, along),
        window(downwind, 4, faces, along),
        window(downwind, 3, faces, along),
        window(downwind, 2, faces, along),
        window(downwind, 1, faces, along),
    )
    face_flux = upper + lower
    return window(face_flux, 0, extent, along) - window(face_flux, 1, extent, along)


def cyclic_rate(upwind, downwind, along):
    upper = weno_face(
        jnp.roll(upwind, 2, axis=along),
        jnp.roll(upwind, 1, axis=along),
        upwind,
        jnp.roll(upwind, -1, axis=along),
        jnp.roll(upwind, -2, axis=along),
    )
    lower = weno_face(
        jnp.roll(downwind, -3, axis=along),
        jnp.roll(downwind, -2, axis=along),
        jnp.roll(downwind, -1, axis=along),
        downwind,
        jnp.roll(downwind, 1, axis=along),
    )
    face_flux = upper + lower
    return jnp.roll(face_flux, 1, axis=along) - face_flux


def tendency(padded, closure):
    wide_x = padded.shape[1] - 6
    wide_y = padded.shape[2] - 6
    along_x = padded[:, :, 3 : 3 + wide_y, :]
    along_y = padded[:, 3 : 3 + wide_x, :, :]
    centre = padded[:, 3 : 3 + wide_x, 3 : 3 + wide_y, :]
    upwind, downwind = split_fluxes(along_x, 0)
    total = axis_rate(upwind, downwind, 1, wide_x)
    upwind, downwind = split_fluxes(along_y, 1)
    total = total + axis_rate(upwind, downwind, 2, wide_y)
    upwind, downwind = split_fluxes(centre, 2)
    total = total + cyclic_rate(upwind, downwind, 3)
    laplace = (
        window(along_x, 2, wide_x, 1)
        + window(along_x, 4, wide_x, 1)
        + (window(along_y, 2, wide_y, 2) + window(along_y, 4, wide_y, 2))
        + (jnp.roll(centre, 1, axis=3) + jnp.roll(centre, -1, axis=3))
        - 6.0 * centre
    )
    viscous = closure[None] * laplace[1:]
    return jnp.concatenate([total[:1], total[1:] + viscous], axis=0)


def scaled_rate(fields, closure_field):
    return TIME_STEP * tendency(fields, closure_field)


def local(state, closure, cotangent):
    wide_x = state.shape[1]
    wide_y = state.shape[2]

    def extend(fields):
        return with_halo(fields, (("gx", 1), ("gy", 2)), 3)

    opening = extend(state)
    states = [state]
    extended = [opening]
    for section_index in range(2):
        rate = tendency(extended[section_index], closure)
        weight_base, weight_section = SECTION_WEIGHTS[section_index]
        after = weight_base * state + weight_section * (states[section_index] + TIME_STEP * rate)
        states.append(after)
        if section_index == 0:
            extended.append(extend(after))
    weight = cotangent
    total = jnp.zeros_like(state)
    grad_closure = jnp.zeros_like(closure)
    for section_index in (2, 1, 0):
        padded = extend(states[section_index])
        weight_base, weight_section = SECTION_WEIGHTS[section_index]
        total = total + weight_base * weight
        scaled = weight_section * weight
        _, pullback = jax.vjp(scaled_rate, padded, closure)
        grad_fields, grad_coeff = pullback(scaled)
        inner = grad_fields[:, 3 : wide_x + 3, 3 : wide_y + 3]
        low_x = grad_fields[:, 0:3, 3 : wide_y + 3]
        high_x = grad_fields[:, wide_x + 3 : wide_x + 6, 3 : wide_y + 3]
        low_y = grad_fields[:, 3 : wide_x + 3, 0:3]
        high_y = grad_fields[:, 3 : wide_x + 3, wide_y + 3 : wide_y + 6]
        from_above_x = passed_along(low_x, "gx", -1)
        from_below_x = passed_along(high_x, "gx", 1)
        from_above_y = passed_along(low_y, "gy", -1)
        from_below_y = passed_along(high_y, "gy", 1)
        inner = inner.at[:, wide_x - 3 :].add(from_above_x)
        inner = inner.at[:, :3].add(from_below_x)
        inner = inner.at[:, :, wide_y - 3 :].add(from_above_y)
        inner = inner.at[:, :, :3].add(from_below_y)
        grad_fields, grad_coeff = (inner, grad_coeff)
        weight = scaled + grad_fields
        grad_closure = grad_closure + grad_coeff
    return (total + weight, grad_closure)


def solution(mesh):
    placed = (
        P("groups", "gx", "gy", None),
        P(("groups", "gx"), "gy", None),
        P("groups", "gx", "gy", None),
    )
    return jax.shard_map(
        local,
        mesh=mesh,
        in_specs=placed,
        out_specs=(P("groups", "gx", "gy", None), P(("groups", "gx"), "gy", None)),
        check_vma=False,
    )
```

profile of v0, /device:TPU:0, one launch (start us, length us, event | category | flops | bytes accessed | tf_op | source)
XLA Modules:
  0.0 149.5 jit_solution(5289470044429952381)
XLA Ops:
  0.6 0.9 fusion.160
  1.6 6.1 %collective-permute-start.1 = (f32[5,3,8,128]{3,2,1,0:T(8,128)S(1)}, f32[5,3,8,128]{3,2,1,0:T(8,128)S(1)}, u32[]{:S(2)}, u32[]{:S(2)}) collective-permute-start(f32[5,3,8,128]{3,2,1,0:T(8,128)S(1)} %get-tuple-element.857), channel_id=1, source_target_pairs={{2,0},{4,2},{6,4},{8,6},{10,8},{12,10},{14,12},{0,14},{3,1},{5,3},... | collective-permute-start | bytes 184328 | tf_op jit(solution)/shard_map/ppermute | solution.py:20
  9.4 5.2 %collective-permute-done = f32[5,3,8,128]{3,2,1,0:T(8,128)S(1)} collective-permute-done((f32[5,3,8,128]{3,2,1,0:T(8,128)S(1)}, f32[5,3,8,128]{3,2,1,0:T(8,128)S(1)}, u32[]{:S(2)}, u32[]{:S(2)}) %collective-permute-start) | collective-permute-done | bytes 61472 | tf_op jit(solution)/shard_map/ppermute | solution.py:18
  17.3 1.8 %divide_add_fusion.5 = (f32[5,4,8,128]{3,2,1,0:T(8,128)S(1)}, f32[5,4,8,128]{3,2,1,0:T(8,128)}, f32[5,4,8,128]{3,2,1,0:T(8,128)}, f32[5,4,8,128]{3,2,1,0:T(8,128...) fusion(f32[5,4,8,128]{3,2,1,0:T(8,128)S(1)} %get-tuple-element., ...), kind=kLoop, calls=%fused_computation.744 | loop fusion | flops 2805760 | bytes 2867200 | tf_op jit(solution)/shard_map/add | solution.py:120
  19.0 1.4 divide_add_fusion.3
  22.7 1.9 %divide_add_fusion.1 = (f32[5,4,9,128]{3,2,1,0:T(8,128)S(1)}, f32[5,4,9,128]{3,2,1,0:T(8,128)}, f32[5,4,9,128]{3,2,1,0:T(8,128)}, f32[5,4,9,128]{3,2,1,0:T(8,128...) fusion(f32[5,4,14,128]{3,2,1,0:T(8,128)S(1)} %get-tuple-element, ...), kind=kLoop, calls=%fused_computation.228 | loop fusion | flops 2972160 | bytes 2672640 | tf_op jit(solution)/shard_map/add | solution.py:101
  28.3 4.7 %collective-permute-start.5 = (f32[5,3,8,128]{3,2,1,0:T(8,128)S(1)}, f32[5,3,8,128]{3,2,1,0:T(8,128)S(1)}, u32[]{:S(2)}, u32[]{:S(2)}) collective-permute-start(f32[5,3,8,128]{3,2,1,0:T(8,128)S(1)} %get-tuple-element.839), channel_id=1, source_target_pairs={{2,0},{4,2},{6,4},{8,6},{10,8},{12,10},{14,12},{0,14},{3,1},{5,3},... | collective-permute-start | bytes 184328 | tf_op jit(solution)/shard_map/ppermute | solution.py:20
  33.0 1.7 %divide_add_fusion.4 = (f32[5,4,8,128]{3,2,1,0:T(8,128)S(1)}, f32[5,4,8,128]{3,2,1,0:T(8,128)}, f32[5,4,8,128]{3,2,1,0:T(8,128)}, f32[5,4,8,128]{3,2,1,0:T(8,128...) fusion(f32[5,4,8,128]{3,2,1,0:T(8,128)S(1)} %get-tuple-element., ...), kind=kLoop, calls=%fused_computation.717 | loop fusion | flops 2805760 | bytes 2867200 | tf_op jit(solution)/shard_map/add | solution.py:120
  37.2 1.5 divide_add_fusion.2
  40.8 2.1 %divide_add_fusion = (f32[5,4,9,128]{3,2,1,0:T(8,128)S(1)}, f32[5,4,9,128]{3,2,1,0:T(8,128)}, f32[5,4,9,128]{3,2,1,0:T(8,128)}, f32[5,4,9,128]{3,2,1,0:T(8,128)}...) fusion(f32[5,4,14,128]{3,2,1,0:T(8,128)S(1)} %get-tuple-element, ...), kind=kLoop, calls=%fused_computation.199 | loop fusion | flops 2972160 | bytes 2672640 | tf_op jit(solution)/shard_map/add | solution.py:101
  44.5 5.0 %collective-permute-start.9 = (f32[5,3,8,128]{3,2,1,0:T(8,128)S(1)}, f32[5,3,8,128]{3,2,1,0:T(8,128)S(1)}, u32[]{:S(2)}, u32[]{:S(2)}) collective-permute-start(f32[5,3,8,128]{3,2,1,0:T(8,128)S(1)} %get-tuple-element.821), channel_id=1, source_target_pairs={{2,0},{4,2},{6,4},{8,6},{10,8},{12,10},{14,12},{0,14},{3,1},{5,3},... | collective-permute-start | bytes 184328 | tf_op jit(solution)/shard_map/ppermute | solution.py:20
  49.8 1.6 %collective-permute-done.8 = f32[5,3,8,128]{3,2,1,0:T(8,128)S(1)} collective-permute-done((f32[5,3,8,128]{3,2,1,0:T(8,128)S(1)}, f32[5,3,8,128]{3,2,1,0:T(8,128)S(1)}, u32[]{:S(2)}, u32[]{:S(2)}) %collective-permute-start.8) | collective-permute-done | bytes 61472 | tf_op jit(solution)/shard_map/ppermute | solution.py:18
  57.2 1.1 negate_add_fusion.5
  64.3 4.9 %collective-permute-start.12 = (f32[5,3,8,128]{3,2,1,0:T(8,128)S(1)}, f32[5,3,8,128]{3,2,1,0:T(8,128)S(1)}, u32[]{:S(2)}, u32[]{:S(2)}) collective-permute-start(f32[5,3,8,128]{3,2,1,0:T(8,128)S(1)} %get-tuple-element.672), channel_id=1, source_target_pairs={{0,14},{2,0},{4,2},{6,4},{8,6},{10,8},{12,10},{14,12},{1,15},{3,1}... | collective-permute-start | bytes 184328 | tf_op jit(solution)/shard_map/ppermute | solution.py:30
  69.3 1.8 %collective-permute-done.12 = f32[5,3,8,128]{3,2,1,0:T(8,128)S(1)} collective-permute-done((f32[5,3,8,128]{3,2,1,0:T(8,128)S(1)}, f32[5,3,8,128]{3,2,1,0:T(8,128)S(1)}, u32[]{:S(2)}, u32[]{:S(2)}) %collective-permute-start.12) | collective-permute-done | bytes 61472 | tf_op jit(solution)/shard_map/ppermute | solution.py:30
  72.4 0.9 scatter-add.44
  73.3 1.4 slice_add_fusion.9
  74.7 0.9 scatter-add.45
  75.7 0.9 broadcast_multiply_fusion
  105.7 4.7 %collective-permute-start.16 = (f32[5,3,8,128]{3,2,1,0:T(8,128)S(1)}, f32[5,3,8,128]{3,2,1,0:T(8,128)S(1)}, u32[]{:S(2)}, u32[]{:S(2)}) collective-permute-start(f32[5,3,8,128]{3,2,1,0:T(8,128)S(1)} %get-tuple-element.668), channel_id=1, source_target_pairs={{0,14},{2,0},{4,2},{6,4},{8,6},{10,8},{12,10},{14,12},{1,15},{3,1}... | collective-permute-start | bytes 184328 | tf_op jit(solution)/shard_map/ppermute | solution.py:30
  110.5 1.8 %collective-permute-done.16 = f32[5,3,8,128]{3,2,1,0:T(8,128)S(1)} collective-permute-done((f32[5,3,8,128]{3,2,1,0:T(8,128)S(1)}, f32[5,3,8,128]{3,2,1,0:T(8,128)S(1)}, u32[]{:S(2)}, u32[]{:S(2)}) %collective-permute-start.16) | collective-permute-done | bytes 61472 | tf_op jit(solution)/shard_map/ppermute | solution.py:30
  130.9 0.8 copy-done.29
  141.3 4.8 %collective-permute-start.20 = (f32[5,3,8,128]{3,2,1,0:T(8,128)S(1)}, f32[5,3,8,128]{3,2,1,0:T(8,128)S(1)}, u32[]{:S(2)}, u32[]{:S(2)}) collective-permute-start(f32[5,3,8,128]{3,2,1,0:T(8,128)S(1)} %get-tuple-element.664), channel_id=1, source_target_pairs={{0,14},{2,0},{4,2},{6,4},{8,6},{10,8},{12,10},{14,12},{1,15},{3,1}... | collective-permute-start | bytes 184328 | tf_op jit(solution)/shard_map/ppermute | solution.py:30
  146.8 1.2 collective-permute-done.20
  (714 shorter events, 87.3 us)
Async XLA Ops:
  1.6 13.8 %collective-permute-start.1 = (f32[5,3,8,128]{3,2,1,0:T(8,128)S(1)}, f32[5,3,8,128]{3,2,1,0:T(8,128)S(1)}, u32[]{:S(2)}, u32[]{:S(2)}) collective-permute-start(f32[5,3,8,128]{3,2,1,0:T(8,128)S(1)} %get-tuple-element.857), channel_id=1, source_target_pairs={{2,0},{4,2},{6,4},{8,6},{10,8},{12,10},{14,12},{0,14},{3,1},{5,3},... | collective-permute-start | bytes 184328 | tf_op jit(solution)/shard_map/ppermute | solution.py:20
  7.6 6.9 %collective-permute-start = (f32[5,3,8,128]{3,2,1,0:T(8,128)S(1)}, f32[5,3,8,128]{3,2,1,0:T(8,128)S(1)}, u32[]{:S(2)}, u32[]{:S(2)}) collective-permute-start(f32[5,3,8,128]{3,2,1,0:T(8,128)S(1)} %get-tuple-element.858), channel_id=1, source_target_pairs={{0,2},{2,4},{4,6},{6,8},{8,10},{10,12},{12,14},{14,0},{1,3},{3,5},... | collective-permute-start | bytes 184328 | tf_op jit(solution)/shard_map/ppermute | solution.py:18
  16.6 3.9 %collective-permute-start.2 = (f32[5,10,3,128]{3,2,1,0:T(4,128)S(1)}, f32[5,10,3,128]{3,2,1,0:T(4,128)S(1)}, u32[]{:S(2)}, u32[]{:S(2)}) collective-permute-start(f32[5,10,3,128]{3,2,1,0:T(4,128)S(1)} %get-tuple-element.722), channel_id=1, source_target_pairs={{0,1},{1,0},{2,3},{3,2},{4,5},{5,4},{6,7},{7,6},{8,9},{9,8},{10,11... | collective-permute-start | bytes 230408 | tf_op jit(solution)/shard_map/ppermute | solution.py:18
  16.7 3.8 %collective-permute-start.3 = (f32[5,10,3,128]{3,2,1,0:T(4,128)S(1)}, f32[5,10,3,128]{3,2,1,0:T(4,128)S(1)}, u32[]{:S(2)}, u32[]{:S(2)}) collective-permute-start(f32[5,10,3,128]{3,2,1,0:T(4,128)S(1)} %get-tuple-element.723), channel_id=1, source_target_pairs={{1,0},{0,1},{3,2},{2,3},{5,4},{4,5},{7,6},{6,7},{9,8},{8,9},{11,10... | collective-permute-start | bytes 230408 | tf_op jit(solution)/shard_map/ppermute | solution.py:20
  28.3 7.0 %collective-permute-start.4 = (f32[5,3,8,128]{3,2,1,0:T(8,128)S(1)}, f32[5,3,8,128]{3,2,1,0:T(8,128)S(1)}, u32[]{:S(2)}, u32[]{:S(2)}) collective-permute-start(f32[5,3,8,128]{3,2,1,0:T(8,128)S(1)} %get-tuple-element.838), channel_id=1, source_target_pairs={{0,2},{2,4},{4,6},{6,8},{8,10},{10,12},{12,14},{14,0},{1,3},{3,5},... | collective-permute-start | bytes 184328 | tf_op jit(solution)/shard_map/ppermute | solution.py:18
  28.3 6.9 %collective-permute-start.5 = (f32[5,3,8,128]{3,2,1,0:T(8,128)S(1)}, f32[5,3,8,128]{3,2,1,0:T(8,128)S(1)}, u32[]{:S(2)}, u32[]{:S(2)}) collective-permute-start(f32[5,3,8,128]{3,2,1,0:T(8,128)S(1)} %get-tuple-element.839), channel_id=1, source_target_pairs={{2,0},{4,2},{6,4},{8,6},{10,8},{12,10},{14,12},{0,14},{3,1},{5,3},... | collective-permute-start | bytes 184328 | tf_op jit(solution)/shard_map/ppermute | solution.py:20
  36.6 2.1 %collective-permute-start.6 = (f32[5,10,3,128]{3,2,1,0:T(4,128)S(1)}, f32[5,10,3,128]{3,2,1,0:T(4,128)S(1)}, u32[]{:S(2)}, u32[]{:S(2)}) collective-permute-start(f32[5,10,3,128]{3,2,1,0:T(4,128)S(1)} %get-tuple-element.720), channel_id=1, source_target_pairs={{0,1},{1,0},{2,3},{3,2},{4,5},{5,4},{6,7},{7,6},{8,9},{9,8},{10,11... | collective-permute-start | bytes 230408 | tf_op jit(solution)/shard_map/ppermute | solution.py:18
  36.7 2.0 %collective-permute-start.7 = (f32[5,10,3,128]{3,2,1,0:T(4,128)S(1)}, f32[5,10,3,128]{3,2,1,0:T(4,128)S(1)}, u32[]{:S(2)}, u32[]{:S(2)}) collective-permute-start(f32[5,10,3,128]{3,2,1,0:T(4,128)S(1)} %get-tuple-element.721), channel_id=1, source_target_pairs={{1,0},{0,1},{3,2},{2,3},{5,4},{4,5},{7,6},{6,7},{9,8},{8,9},{11,10... | collective-permute-start | bytes 230408 | tf_op jit(solution)/shard_map/ppermute | solution.py:20
  44.5 7.0 %collective-permute-start.8 = (f32[5,3,8,128]{3,2,1,0:T(8,128)S(1)}, f32[5,3,8,128]{3,2,1,0:T(8,128)S(1)}, u32[]{:S(2)}, u32[]{:S(2)}) collective-permute-start(f32[5,3,8,128]{3,2,1,0:T(8,128)S(1)} %get-tuple-element.820), channel_id=1, source_target_pairs={{0,2},{2,4},{4,6},{6,8},{8,10},{10,12},{12,14},{14,0},{1,3},{3,5},... | collective-permute-start | bytes 184328 | tf_op jit(solution)/shard_map/ppermute | solution.py:18
  44.5 7.0 %collective-permute-start.9 = (f32[5,3,8,128]{3,2,1,0:T(8,128)S(1)}, f32[5,3,8,128]{3,2,1,0:T(8,128)S(1)}, u32[]{:S(2)}, u32[]{:S(2)}) collective-permute-start(f32[5,3,8,128]{3,2,1,0:T(8,128)S(1)} %get-tuple-element.821), channel_id=1, source_target_pairs={{2,0},{4,2},{6,4},{8,6},{10,8},{12,10},{14,12},{0,14},{3,1},{5,3},... | collective-permute-start | bytes 184328 | tf_op jit(solution)/shard_map/ppermute | solution.py:20
  51.7 1.4 collective-permute-start.10
  51.8 1.4 collective-permute-start.11
  63.7 9.6 %collective-permute-start.15 = (f32[5,4,3,128]{3,2,1,0:T(4,128)}, f32[5,4,3,128]{3,2,1,0:T(4,128)}, u32[]{:S(2)}, u32[]{:S(2)}) collective-permute-start(f32[5,4,3,128]{3,2,1,0:T(4,128)} %get-tuple-element.669), channel_id=1, source_target_pairs={{0,1},{1,0},{2,3},{3,2},{4,5},{5,4},{6,7},{7,6},{8,9},{9,8},{10,11... | collective-permute-start | bytes 92168 | tf_op jit(solution)/shard_map/ppermute | solution.py:30
  64.1 7.6 %collective-permute-start.14 = (f32[5,4,3,128]{3,2,1,0:T(4,128)S(1)}, f32[5,4,3,128]{3,2,1,0:T(4,128)S(1)}, u32[]{:S(2)}, u32[]{:S(2)}) collective-permute-start(f32[5,4,3,128]{3,2,1,0:T(4,128)S(1)} %get-tuple-element.670), channel_id=1, source_target_pairs={{0,1},{1,0},{2,3},{3,2},{4,5},{5,4},{6,7},{7,6},{8,9},{9,8},{10,11... | collective-permute-start | bytes 92168 | tf_op jit(solution)/shard_map/ppermute | solution.py:30
  64.3 7.4 %collective-permute-start.13 = (f32[5,3,8,128]{3,2,1,0:T(8,128)S(1)}, f32[5,3,8,128]{3,2,1,0:T(8,128)S(1)}, u32[]{:S(2)}, u32[]{:S(2)}) collective-permute-start(f32[5,3,8,128]{3,2,1,0:T(8,128)S(1)} %get-tuple-element.671), channel_id=1, source_target_pairs={{0,2},{2,4},{4,6},{6,8},{8,10},{10,12},{12,14},{14,0},{1,3},{3,5},... | collective-permute-start | bytes 184328 | tf_op jit(solution)/shard_map/ppermute | solution.py:30
  64.3 6.8 %collective-permute-start.12 = (f32[5,3,8,128]{3,2,1,0:T(8,128)S(1)}, f32[5,3,8,128]{3,2,1,0:T(8,128)S(1)}, u32[]{:S(2)}, u32[]{:S(2)}) collective-permute-start(f32[5,3,8,128]{3,2,1,0:T(8,128)S(1)} %get-tuple-element.672), channel_id=1, source_target_pairs={{0,14},{2,0},{4,2},{6,4},{8,6},{10,8},{12,10},{14,12},{1,15},{3,1}... | collective-permute-start | bytes 184328 | tf_op jit(solution)/shard_map/ppermute | solution.py:30
  105.1 7.7 %collective-permute-start.19 = (f32[5,4,3,128]{3,2,1,0:T(4,128)S(1)}, f32[5,4,3,128]{3,2,1,0:T(4,128)S(1)}, u32[]{:S(2)}, u32[]{:S(2)}) collective-permute-start(f32[5,4,3,128]{3,2,1,0:T(4,128)S(1)} %get-tuple-element.665), channel_id=1, source_target_pairs={{0,1},{1,0},{2,3},{3,2},{4,5},{5,4},{6,7},{7,6},{8,9},{9,8},{10,11... | collective-permute-start | bytes 92168 | tf_op jit(solution)/shard_map/ppermute | solution.py:30
  105.2 7.4 %collective-permute-start.18 = (f32[5,4,3,128]{3,2,1,0:T(4,128)S(1)}, f32[5,4,3,128]{3,2,1,0:T(4,128)S(1)}, u32[]{:S(2)}, u32[]{:S(2)}) collective-permute-start(f32[5,4,3,128]{3,2,1,0:T(4,128)S(1)} %get-tuple-element.666), channel_id=1, source_target_pairs={{0,1},{1,0},{2,3},{3,2},{4,5},{5,4},{6,7},{7,6},{8,9},{9,8},{10,11... | collective-permute-start | bytes 92168 | tf_op jit(solution)/shard_map/ppermute | solution.py:30
  105.7 6.9 %collective-permute-start.17 = (f32[5,3,8,128]{3,2,1,0:T(8,128)S(1)}, f32[5,3,8,128]{3,2,1,0:T(8,128)S(1)}, u32[]{:S(2)}, u32[]{:S(2)}) collective-permute-start(f32[5,3,8,128]{3,2,1,0:T(8,128)S(1)} %get-tuple-element.667), channel_id=1, source_target_pairs={{0,2},{2,4},{4,6},{6,8},{8,10},{10,12},{12,14},{14,0},{1,3},{3,5},... | collective-permute-start | bytes 184328 | tf_op jit(solution)/shard_map/ppermute | solution.py:30
  105.7 6.6 %collective-permute-start.16 = (f32[5,3,8,128]{3,2,1,0:T(8,128)S(1)}, f32[5,3,8,128]{3,2,1,0:T(8,128)S(1)}, u32[]{:S(2)}, u32[]{:S(2)}) collective-permute-start(f32[5,3,8,128]{3,2,1,0:T(8,128)S(1)} %get-tuple-element.668), channel_id=1, source_target_pairs={{0,14},{2,0},{4,2},{6,4},{8,6},{10,8},{12,10},{14,12},{1,15},{3,1}... | collective-permute-start | bytes 184328 | tf_op jit(solution)/shard_map/ppermute | solution.py:30
  140.7 7.8 %collective-permute-start.23 = (f32[5,4,3,128]{3,2,1,0:T(4,128)S(1)}, f32[5,4,3,128]{3,2,1,0:T(4,128)S(1)}, u32[]{:S(2)}, u32[]{:S(2)}) collective-permute-start(f32[5,4,3,128]{3,2,1,0:T(4,128)S(1)} %get-tuple-element.661), channel_id=1, source_target_pairs={{0,1},{1,0},{2,3},{3,2},{4,5},{5,4},{6,7},{7,6},{8,9},{9,8},{10,11... | collective-permute-start | bytes 92168 | tf_op jit(solution)/shard_map/ppermute | solution.py:30
  140.8 7.5 %collective-permute-start.22 = (f32[5,4,3,128]{3,2,1,0:T(4,128)S(1)}, f32[5,4,3,128]{3,2,1,0:T(4,128)S(1)}, u32[]{:S(2)}, u32[]{:S(2)}) collective-permute-start(f32[5,4,3,128]{3,2,1,0:T(4,128)S(1)} %get-tuple-element.662), channel_id=1, source_target_pairs={{0,1},{1,0},{2,3},{3,2},{4,5},{5,4},{6,7},{7,6},{8,9},{9,8},{10,11... | collective-permute-start | bytes 92168 | tf_op jit(solution)/shard_map/ppermute | solution.py:30
  141.3 7.0 %collective-permute-start.21 = (f32[5,3,8,128]{3,2,1,0:T(8,128)S(1)}, f32[5,3,8,128]{3,2,1,0:T(8,128)S(1)}, u32[]{:S(2)}, u32[]{:S(2)}) collective-permute-start(f32[5,3,8,128]{3,2,1,0:T(8,128)S(1)} %get-tuple-element.663), channel_id=1, source_target_pairs={{0,2},{2,4},{4,6},{6,8},{8,10},{10,12},{12,14},{14,0},{1,3},{3,5},... | collective-permute-start | bytes 184328 | tf_op jit(solution)/shard_map/ppermute | solution.py:30
  141.3 6.6 %collective-permute-start.20 = (f32[5,3,8,128]{3,2,1,0:T(8,128)S(1)}, f32[5,3,8,128]{3,2,1,0:T(8,128)S(1)}, u32[]{:S(2)}, u32[]{:S(2)}) collective-permute-start(f32[5,3,8,128]{3,2,1,0:T(8,128)S(1)} %get-tuple-element.664), channel_id=1, source_target_pairs={{0,14},{2,0},{4,2},{6,4},{8,6},{10,8},{12,10},{14,12},{1,15},{3,1}... | collective-permute-start | bytes 184328 | tf_op jit(solution)/shard_map/ppermute | solution.py:30
  (192 other events, 204.8 us)
where the time goes:
time: 152 us; the launch traced here: 149 us
  local copies, waits for them, and re-layouts  55.9 us (37%)
  other arithmetic  42.6 us (28%)
  starting transfers between devices  33.7 us (22%)
  waiting for transfers between devices  14.1 us (9%)
  between operations  3.17 us (2%)
    unnamed x394, local copies, waits for them, and re-layouts  46.9 us
    ppermute x6, starting transfers between devices, with_halo(): lax.ppermute(head, axis, [((i + 1) % count, i) for i in range(count)])  17.2 us
    ppermute x12, starting transfers between devices, passed_along(): return lax.ppermute(value, axis, pairs)  16.1 us
    ppermute x6, waiting for transfers between devices, with_halo(): lax.ppermute(tail, axis, [(i, (i + 1) % count) for i in range(count)])  7.91 us
    add x4, other arithmetic, axis_rate(): face_flux = upper + lower  6.83 us
    add_any x32, other arithmetic, weno_face(): cand_zero = (2.0 * left_two - 7.0 * left_one + 11.0 * centre) / 6.0  6.25 us
    ppermute x12, waiting for transfers between devices, passed_along(): return lax.ppermute(value, axis, pairs)  6.01 us
    add_any x15, other arithmetic, weno_face(): cand_two = (2.0 * centre + 5.0 * right_one - right_two) / 6.0  4.51 us
  transfers between devices with their start and end apart: 24, of which 11 were waited for; matrix products, arithmetic and copies ran while one was open for 8% of the time, Pallas kernels for 0%

commit v1 on v0

v1 whole, which is shorter than its diff:
```python
import functools
import jax
import jax.numpy as jnp
from jax import lax
from jax.experimental import pallas as pl
from jax.experimental.pallas import tpu as pltpu
from jax.sharding import PartitionSpec as P

WENO_EPS = 1e-06
TIME_STEP = 0.06
SECTION_WEIGHTS = ((0.0, 1.0), (0.75, 0.25), (1.0 / 3.0, 2.0 / 3.0))
HALO = 3
MESH = pl.DeviceIdType.MESH


def inverse_of(value):
    return 1.0 / value


def shifted(value, steps, axis):
    return pltpu.roll(value, (-steps) % value.shape[axis], axis)


def cell_terms(q, direction):
    inverse = inverse_of(q[0])
    squares = q[1] * q[1] + q[2] * q[2] + q[3] * q[3]
    pressure = 0.4 * (q[4] - 0.5 * squares * inverse)
    speed = q[1 + direction] * inverse
    inside = speed * speed + 1.4 * pressure * inverse
    root = lax.rsqrt(inside)
    return inverse, squares, pressure, speed, 1.5 * inside * root, root


def split_fluxes(q, direction):
    _, _, pressure, speed, wave, _ = cell_terms(q, direction)
    flux = [q[1 + direction], q[1] * speed, q[2] * speed, q[3] * speed, (q[4] + pressure) * speed]
    flux[1 + direction] = flux[1 + direction] + pressure
    half = 0.5 * wave
    up, down = [], []
    for c in range(5):
        centre, spread = 0.5 * flux[c], half * q[c]
        up.append(centre + spread)
        down.append(centre - spread)
    return up, down


def split_fluxes_back(q, up, down, direction):
    inverse, squares, pressure, speed, wave, root = cell_terms(q, direction)
    flux = [0.5 * (up[c] + down[c]) for c in range(5)]
    diff = [0.5 * (up[c] - down[c]) for c in range(5)]
    grad = [wave * diff[c] for c in range(5)]
    wave_bar = diff[0] * q[0] + diff[1] * q[1] + diff[2] * q[2] + diff[3] * q[3] + diff[4] * q[4]
    wave_bar = (1.5 * wave_bar) * root
    lift = flux[4] * speed
    ratio_bar = 0.7 * wave_bar
    speed_bar = (
        flux[1] * q[1] + flux[2] * q[2] + flux[3] * q[3]
        + flux[4] * (q[4] + pressure) + wave_bar * speed
    )
    pressure_bar = flux[1 + direction] + lift + ratio_bar * inverse
    inverse_bar = ratio_bar * pressure + speed_bar * q[1 + direction] - (0.2 * pressure_bar) * squares
    slope = 0.4 * pressure_bar
    pull = slope * inverse
    for k in range(1, 4):
        grad[k] = grad[k] + flux[k] * speed - pull * q[k]
    grad[1 + direction] = grad[1 + direction] + flux[0] + speed_bar * inverse
    grad[4] = grad[4] + lift + slope
    grad[0] = grad[0] - inverse_bar * inverse * inverse
    return grad


def rough(bend):
    return WENO_EPS + (13.0 / 12.0) * bend * bend


def weno(centre, d1, d2, s0, s1, s2, m0, m1, m2, sign):
    half = 0.5 * sign
    t0, t1, t2 = d1 + half * s0, d1 + half * s1, d2 - half * s2
    r0, r1, r2 = inverse_of(m0 + t0 * t0), inverse_of(m1 + t1 * t1), inverse_of(m2 + t2 * t2)
    w0, w1, w2 = r0 * r0, 6.0 * (r1 * r1), 3.0 * (r2 * r2)
    scale = inverse_of(w0 + w1 + w2)
    w0, w1, w2 = w0 * scale, w1 * scale, w2 * scale
    e0, e1 = (1.0 / 3.0) * s0, (1.0 / 3.0) * s1
    e2 = 0.5 * s1 - (1.0 / 6.0) * s2
    mean = w0 * e0 + w1 * e1 + w2 * e2
    face = centre + half * d1 + mean
    c0 = w0 * r0 * (mean - e0)
    c1 = w1 * r1 * (mean - e1)
    c2 = w2 * r2 * (mean - e2)
    c0, c1, c2 = c0 + c0, c1 + c1, c2 + c2
    k = 13.0 / 6.0
    p0, p1, p2 = c0 * t0, c1 * t1, c2 * t2
    third = 1.0 / 3.0
    if sign > 0:
        a0 = third * w0 + k * (c0 * s0) + p0
        a1 = third * w1 + 0.5 * w2 + k * (c1 * s1) + p1
        a2 = k * (c2 * s2) - (1.0 / 6.0) * w2 - p2
    else:
        a0 = third * w0 + k * (c0 * s0) - p0
        a1 = third * w1 + 0.5 * w2 + k * (c1 * s1) - p1
        a2 = k * (c2 * s2) - (1.0 / 6.0) * w2 + p2
    g1 = half + 2.0 * (p0 + p1)
    g2 = 2.0 * p2
    return face, (a0, a1, a2, g1, g2)


def ring_weno(f, axis, sign):
    ahead = shifted(f, 1, axis) - f
    behind = shifted(ahead, -1, axis)
    bend = ahead - behind
    m = rough(bend)
    below, above = shifted(bend, -1, axis), shifted(bend, 1, axis)
    if sign > 0:
        return weno(f, behind, ahead, below, bend, above, rough(below), m, rough(above), 1.0)
    return weno(f, ahead, behind, above, bend, below, rough(above), m, rough(below), -1.0)


def ring_weno_back(mu, coef, axis, sign):
    a0, a1, a2, g1, g2 = [k * mu for k in coef]
    if sign > 0:
        bend = shifted(a0, 1, axis) + a1 + shifted(a2, -1, axis)
        ahead = g2 + bend + shifted(g1 - bend, 1, axis)
    else:
        bend = shifted(a0, -1, axis) + a1 + shifted(a2, 1, axis)
        ahead = g1 + bend + shifted(g2 - bend, 1, axis)
    return mu + shifted(ahead, -1, axis) - ahead


def plus(total, term):
    return term if total is None else total + term


def kernel(
    n, state, closure, cotangent, out_state, out_closure,
    q, other, coef_x, coef_y, coef_z, lap, fx, fy, fz, rate,
    lam, weight, total, gx, go, gin, rx_low, rx_high, ro, send, recv,
):
    wide = n + 2 * HALO
    mine = pl.ds(HALO, n)
    count = lax.axis_size("gx")
    me = lax.axis_index("gx")
    right, left = lax.rem(me + 1, count), lax.rem(me + count - 1, count)
    across = 1 - lax.axis_index("gy")
    barrier = pltpu.get_barrier_semaphore()
    for target in ({"gx": left}, {"gx": right}, {"gy": across}):
        pl.semaphore_signal(barrier, inc=1, device_id=target, device_id_type=MESH)

    q[0, :, mine] = state[...]
    pl.semaphore_wait(barrier, 3)

    def three(number, sources, targets):
        made = []
        for k, (source, landing, target) in enumerate(
            zip(sources, targets, ({"gx": left}, {"gx": right}, {"gy": across}))
        ):
            made.append(
                pltpu.make_async_remote_copy(
                    src_ref=source, dst_ref=landing,
                    send_sem=send.at[number, k], recv_sem=recv.at[number, k],
                    device_id=target, device_id_type=MESH,
                )
            )
        return made

    pending = []

    def each(body, length=5):
        def step(i, carry):
            body(i)
            return carry
        lax.fori_loop(0, length, step, 0)

    def ring_y(s, c):
        return jnp.concatenate([q[s, c, mine], other[s, c]], axis=1)

    def forward(s):
        last = s == 2
        copies = three(
            s,
            (q.at[s, :, pl.ds(HALO, HALO)], q.at[s, :, pl.ds(n, HALO)], q.at[s, :, mine]),
            (q.at[s, :, pl.ds(n + HALO, HALO)], q.at[s, :, pl.ds(0, HALO)], other.at[s]),
        )
        for copy in (copies[2], copies[0], copies[1]):
            copy.start()
        pending.extend(copies)

        up, down = split_fluxes([q[s, c, mine] for c in range(5)], 2)
        for c in range(5):
            fz[0, c] = up[c]
            fz[1, c] = down[c]

        def along_z(c):
            face, coef = ring_weno(fz[0, c], 2, 1)
            face_low, coef_low = ring_weno(fz[1, c], 2, -1)
            for k in range(5):
                coef_z[s, c, 0, k] = coef[k]
                coef_z[s, c, 1, k] = coef_low[k]
            if not last:
                face = face + shifted(face_low, 1, 2)
                rate[c] = shifted(face, -1, 2) - face
            own = q[s, c, mine]
            lap[s, c] = shifted(own, -1, 2) + shifted(own, 1, 2) - 6.0 * own

        each(along_z)
        copies[2].wait_recv()
        up, down = split_fluxes([ring_y(s, c) for c in range(5)], 1)
        for c in range(5):
            fy[0, c] = up[c]
            fy[1, c] = down[c]

        def along_y(c):
            face, coef = ring_weno(fy[0, c], 1, 1)
            face_low, coef_low = ring_weno(fy[1, c], 1, -1)
            for k in range(5):
                coef_y[s, c, 0, k] = coef[k]
                coef_y[s, c, 1, k] = coef_low[k]
            if not last:
                face = face + shifted(face_low, 1, 1)
                rate[c] += (shifted(face, -1, 1) - face)[:, :8]
            both = ring_y(s, c)
            lap[s, c] += (shifted(both, -1, 1) + shifted(both, 1, 1))[:, :8]

        each(along_y)
        copies[0].wait_recv()
        copies[1].wait_recv()

        def flux_x(i):
            at = pl.ds(2 * i, 2)
            up, down = split_fluxes([q[s, c, at] for c in range(5)], 0)
            for c in range(5):
                fx[0, c, at] = up[c]
                fx[1, c, at] = down[c]

        each(flux_x, wide // 2)
        weight_base, weight_section = SECTION_WEIGHTS[s]

        def along_x(c):
            faces = [None] * (n + 1)
            for side, sign in ((0, 1), (1, -1)):
                f = [fx[side, c, i] for i in range(wide)]
                d = [f[i + 1] - f[i] for i in range(wide - 1)]
                bend = [None] + [d[i] - d[i - 1] for i in range(1, wide - 1)]
                m = [None] + [rough(b) for b in bend[1:]]
                for face in range(n + 1):
                    if sign > 0:
                        i = face + 2
                        value, coef = weno(
                            f[i], d[i - 1], d[i], bend[i - 1], bend[i], bend[i + 1],
                            m[i - 1], m[i], m[i + 1], 1.0)
                    else:
                        i = face + 3
                        value, coef = weno(
                            f[i], d[i], d[i - 1], bend[i + 1], bend[i], bend[i - 1],
                            m[i + 1], m[i], m[i - 1], -1.0)
                    faces[face] = plus(faces[face], value)
                    for k in range(5):
                        coef_x[s, c, side, k, face] = coef[k]
            on = jnp.where(c > 0, 1.0, 0.0)
            for x in range(n):
                i = x + HALO
                whole = lap[s, c, x] + q[s, c, i - 1] + q[s, c, i + 1]
                whole = whole * on
                lap[s, c, x] = whole
                if not last:
                    speed = rate[c, x] + (faces[x] - faces[x + 1]) + closure[x] * whole
                    q[s + 1, c, i] = (
                        weight_base * q[0, c, i] + weight_section * (q[s, c, i] + TIME_STEP * speed)
                    )

        each(along_x)

    def backward(s):
        weight_base, weight_section = SECTION_WEIGHTS[s]

        def along_x(c):
            on = jnp.where(c > 0, 1.0, 0.0)
            load = []
            for x in range(n):
                here = weight[c, x]
                total[c, x] += weight_base * here
                load.append((TIME_STEP * weight_section) * here)
                lam[c, x] = load[x]
                gin[c, x] = weight_section * here
            mus = [load[0]] + [load[x] - load[x - 1] for x in range(1, n)] + [-load[n - 1]]
            for side, sign in ((0, 1), (1, -1)):
                bend = [None] * wide
                ahead = [None] * wide
                value = [None] * wide
                for face in range(n + 1):
                    mu = mus[face]
                    a0, a1, a2, g1, g2 = [coef_x[s, c, side, k, face] * mu for k in range(5)]
                    i = face + 2 if sign > 0 else face + 3
                    value[i] = mu
                    bend[i] = plus(bend[i], a1)
                    bend[i - sign] = plus(bend[i - sign], a0)
                    bend[i + sign] = plus(bend[i + sign], a2)
                    first, second = (i - 1, i) if sign > 0 else (i, i - 1)
                    ahead[first] = plus(ahead[first], g1)
                    ahead[second] = plus(ahead[second], g2)
                for i in range(wide):
                    if bend[i] is not None:
                        ahead[i] = plus(ahead[i], bend[i])
                        ahead[i - 1] = plus(ahead[i - 1], -bend[i])
                for i in range(wide):
                    if ahead[i] is not None:
                        value[i + 1] = plus(value[i + 1], ahead[i])
                        value[i] = plus(value[i], -ahead[i])
                for i in range(wide):
                    fx[side, c, i] = jnp.zeros_like(mus[0]) if value[i] is None else value[i]
            kappa = [on * closure[x] * load[x] for x in range(n)]
            for i in range(wide):
                x = i - HALO
                term = None
                if 0 <= x - 1 < n:
                    term = plus(term, kappa[x - 1])
                if 0 <= x + 1 < n:
                    term = plus(term, kappa[x + 1])
                if 0 <= x < n:
                    term = plus(term, -6.0 * kappa[x])
                gx[s, c, i] = jnp.zeros_like(mus[0]) if term is None else term

        each(along_x)

        def pull_x(i):
            at = pl.ds(2 * i, 2)
            grad = split_fluxes_back(
                [q[s, c, at] for c in range(5)],
                [fx[0, c, at] for c in range(5)],
                [fx[1, c, at] for c in range(5)], 0)
            for c in range(5):
                gx[s, c, at] += grad[c]

        each(pull_x, wide // 2)
        copies = three(
            HALO + s,
            (gx.at[s, :, pl.ds(0, HALO)], gx.at[s, :, pl.ds(n + HALO, HALO)], go.at[s]),
            (rx_high.at[s], rx_low.at[s], ro.at[s]),
        )
        copies[0].start()
        copies[1].start()

        def along_y(c):
            on = jnp.where(c > 0, 1.0, 0.0)
            own = lam[c]
            ring = jnp.concatenate([own, jnp.zeros_like(own)], axis=1)
            mu = shifted(ring, 1, 1) - ring
            nu = ring - shifted(ring, -1, 1)
            fy[0, c] = ring_weno_back(mu, [coef_y[s, c, 0, k] for k in range(5)], 1, 1)
            fy[1, c] = ring_weno_back(nu, [coef_y[s, c, 1, k] for k in range(5)], 1, -1)
            kappa = own * closure[...] * on
            ring = jnp.concatenate([kappa, jnp.zeros_like(own)], axis=1)
            both = shifted(ring, 1, 1) + shifted(ring, -1, 1)
            gin[c] += both[:, :8] + shifted(kappa, 1, 2) + shifted(kappa, -1, 2)
            go[s, c] = both[:, 8:]

        each(along_y)

        def pull_y(x):
            grad = split_fluxes_back(
                [jnp.concatenate([q[s, c, x + HALO], other[s, c, x]], axis=0) for c in range(5)],
                [fy[0, c, x] for c in range(5)],
                [fy[1, c, x] for c in range(5)], 1)
            for c in range(5):
                gin[c, x] += grad[c][:8]
                go[s, c, x] += grad[c][8:]

        each(pull_y, n)
        copies[2].start()
        pending.extend(copies)

        def along_z(c):
            own = lam[c]
            mu = shifted(own, 1, 2) - own
            nu = own - shifted(own, -1, 2)
            fz[0, c] = ring_weno_back(mu, [coef_z[s, c, 0, k] for k in range(5)], 2, 1)
            fz[1, c] = ring_weno_back(nu, [coef_z[s, c, 1, k] for k in range(5)], 2, -1)

        each(along_z)

        def pull_z(i):
            at = pl.ds(2 * i, 2)
            inner = pl.ds(2 * i + HALO, 2)
            grad = split_fluxes_back(
                [q[s, c, inner] for c in range(5)],
                [fz[0, c, at] for c in range(5)],
                [fz[1, c, at] for c in range(5)], 2)
            for c in range(5):
                gin[c, at] += grad[c] + gx[s, c, inner]

        each(pull_z, n // 2)
        share = lam[1] * lap[s, 1]
        for c in range(2, 5):
            share = share + lam[c] * lap[s, c]
        out_closure[...] = share if s == 2 else out_closure[...] + share
        for copy in copies:
            copy.wait_recv()

        def gather(c):
            weight[c] = gin[c] + ro[s, c]
            weight[c, pl.ds(n - HALO, HALO)] += rx_high[s, c]
            weight[c, pl.ds(0, HALO)] += rx_low[s, c]

        each(gather)

    for s in range(3):
        forward(s)
    weight[...] = cotangent[...]
    total[...] = jnp.zeros_like(total)
    for s in (2, 1, 0):
        backward(s)
    out_state[...] = total[...] + weight[...]
    for copy in pending:
        copy.wait_send()


def local(state, closure, cotangent):
    _, n, rows, lanes = state.shape
    f32 = jnp.float32
    wide = n + 2 * HALO
    plane = (rows, lanes)

    def vmem(*shape):
        return pltpu.VMEM(shape + plane, f32)

    def tall(*shape):
        return pltpu.VMEM(shape + (2 * rows, lanes), f32)

    return pl.pallas_call(
        functools.partial(kernel, n),
        out_shape=(
            jax.ShapeDtypeStruct(state.shape, f32),
            jax.ShapeDtypeStruct(closure.shape, f32),
        ),
        in_specs=[pl.BlockSpec(memory_space=pltpu.VMEM)] * 3,
        out_specs=(pl.BlockSpec(memory_space=pltpu.VMEM),) * 2,
        scratch_shapes=[
            vmem(3, 5, wide), vmem(3, 5, n),
            vmem(3, 5, 2, 5, n + 1), tall(3, 5, 2, 5, n), vmem(3, 5, 2, 5, n),
            vmem(3, 5, n), vmem(2, 5, wide), tall(2, 5, n), vmem(2, 5, n), vmem(5, n),
            vmem(5, n), vmem(5, n), vmem(5, n),
            vmem(3, 5, wide), vmem(3, 5, n), vmem(5, n),
            vmem(3, 5, HALO), vmem(3, 5, HALO), vmem(3, 5, n),
            pltpu.SemaphoreType.DMA((6, 3)), pltpu.SemaphoreType.DMA((6, 3)),
        ],
        compiler_params=pltpu.CompilerParams(
            collective_id=0, has_side_effects=True, vmem_limit_bytes=40 * 1024 * 1024
        ),
    )(state, closure, cotangent)


def solution(mesh):
    placed = (
        P("groups", "gx", "gy", None),
        P(("groups", "gx"), "gy", None),
        P("groups", "gx", "gy", None),
    )
    return jax.shard_map(
        local,
        mesh=mesh,
        in_specs=placed,
        out_specs=(P("groups", "gx", "gy", None), P(("groups", "gx"), "gy", None)),
        check_vma=False,
    )
```

time: 152 us -> 42 us (0.28); the launches traced: 149 us -> 41.7 us
  local copies, waits for them, and re-layouts: 55.9 us -> 3.73 us
  other arithmetic: 42.6 us -> 0 us
  Pallas kernels: 0 us -> 37.4 us
  starting transfers between devices: 33.7 us -> 0 us
  waiting for transfers between devices: 14.1 us -> 0 us
  between operations: 3.17 us -> 0.65 us
    unnamed x394 -> x8, local copies, waits for them, and re-layouts: 46.9 us -> 3.73 us
    pallas_call x0 -> x1, Pallas kernels: none -> 37.4 us  [local(): pl.pallas_call(functools.partial(kernel, n), out_shape=(jax.ShapeDtypeStr...]
    ppermute x24 -> x0, starting transfers between devices: 33.7 us -> none  [the longest x6 17.2 us: with_halo(): lax.ppermute(head, axis, [((i + 1) % count, i) for i in range(count)])]
    add_any x86 -> x0, other arithmetic: 15.9 us -> none  [the longest x32 6.25 us: weno_face(): cand_zero = (2.0 * left_two - 7.0 * left_one + 11.0 * centre) / 6.0]
    add x20 -> x0, other arithmetic: 15.4 us -> none  [the longest x4 6.83 us: axis_rate(): face_flux = upper + lower]
    ppermute x24 -> x0, waiting for transfers between devices: 14.1 us -> none  [the longest x6 7.91 us: with_halo(): lax.ppermute(tail, axis, [(i, (i + 1) % count) for i in range(count)])]
    mul x39 -> x0, other arithmetic: 6.33 us -> none  [the longest x12 4.27 us: split_fluxes(): upwind = 0.5 * (fluxes + wave_speed * fields)]
    slice x43 -> x0, local copies, waits for them, and re-layouts: 3.74 us -> none  [the longest x1 0.94 us: with_halo(): head = lax.slice_in_dim(cells, 0, width, axis=dim)]
  transfers between devices with their start and end apart: 24 -> 0, of which waited for: 11 -> 0; matrix products, arithmetic and copies ran while one was open for 8% -> 0% of each run, Pallas kernels for 0% -> 0%
where the time goes in v1:
time: 42 us; the launch traced here: 41.7 us
  Pallas kernels  37.4 us (89%)
  local copies, waits for them, and re-layouts  3.73 us (9%)
  between operations  0.65 us (2%)
    pallas_call x1, Pallas kernels, local(): pl.pallas_call(functools.partial(kernel, n), out_shape=(jax.ShapeDtypeStr...  37.4 us
    unnamed x8, local copies, waits for them, and re-layouts  3.73 us

profile of v1, /device:TPU:0, one launch (start us, length us, event | category | flops | bytes accessed | tf_op | source)
XLA Modules:
  0.0 41.7 jit_solution(4336150395417214868)
XLA Ops:
  0.6 0.0 copy-start
  0.6 0.9 %copy-done = f32[5,4,8,128]{3,2,1,0:T(8,128)S(1)} copy-done((f32[5,4,8,128]{3,2,1,0:T(8,128)S(1)}, f32[5,4,8,128]{3,2,1,0:T(8,128)}, u32[]{:S(2)}) %copy-start) | copy-done | bytes 81944
  1.5 0.0 copy-start.1
  1.5 0.9 %copy-done.1 = f32[5,4,8,128]{3,2,1,0:T(8,128)S(1)} copy-done((f32[5,4,8,128]{3,2,1,0:T(8,128)S(1)}, f32[5,4,8,128]{3,2,1,0:T(8,128)}, u32[]{:S(2)}) %copy-start.1) | copy-done | bytes 81944
  2.4 0.0 copy-start.2
  2.4 0.7 %copy-done.2 = f32[4,8,128]{2,1,0:T(8,128)S(1)} copy-done((f32[4,8,128]{2,1,0:T(8,128)S(1)}, f32[4,8,128]{2,1,0:T(8,128)}, u32[]{:S(2)}) %copy-start.2) | copy-done | bytes 16408
  3.1 37.4 %shard_map.50 = (f32[5,4,8,128]{3,2,1,0:T(8,128)S(1)}, f32[4,8,128]{2,1,0:T(8,128)S(1)}) custom-call(f32[5,4,8,128]{3,2,1,0:T(8,128)S(1)} %copy-done, f32[4,8,128]{2,1,0:T(8,128)S(1)} %copy-done.2, f32[5,4,8,128]{3,2,1,0:T(8,128)S(1)} %copy-done.1), custom_call_target="tpu_custom_call" | custom-call | tf_op jit(solution)/shard_map/pallas_call | solution.py:428
  40.5 0.6 %copy.7 = f32[5,4,8,128]{3,2,1,0:T(8,128)} copy(f32[5,4,8,128]{3,2,1,0:T(8,128)S(1)} %get-tuple-element.4) | data formatting | bytes 163840
  41.1 0.6 %copy.8 = f32[4,8,128]{2,1,0:T(8,128)} copy(f32[4,8,128]{2,1,0:T(8,128)S(1)} %get-tuple-element.5) | data formatting | bytes 32768
Async XLA Ops:
  0.6 0.9 %copy-start = (f32[5,4,8,128]{3,2,1,0:T(8,128)S(1)}, f32[5,4,8,128]{3,2,1,0:T(8,128)}, u32[]{:S(2)}) copy-start(f32[5,4,8,128]{3,2,1,0:T(8,128)} %state.1) | copy-start | bytes 245764
  1.5 0.9 %copy-start.1 = (f32[5,4,8,128]{3,2,1,0:T(8,128)S(1)}, f32[5,4,8,128]{3,2,1,0:T(8,128)}, u32[]{:S(2)}) copy-start(f32[5,4,8,128]{3,2,1,0:T(8,128)} %cotangent.1) | copy-start | bytes 245764
  2.4 0.7 %copy-start.2 = (f32[4,8,128]{2,1,0:T(8,128)S(1)}, f32[4,8,128]{2,1,0:T(8,128)}, u32[]{:S(2)}) copy-start(f32[4,8,128]{2,1,0:T(8,128)} %closure.1) | copy-start | bytes 49156

commit v2 on v1

--- a/solution.py
+++ b/solution.py
@@ -74,56 +74,48 @@
 
 
 def weno(centre, d1, d2, s0, s1, s2, m0, m1, m2, sign):
-    half = 0.5 * sign
-    t0, t1, t2 = d1 + half * s0, d1 + half * s1, d2 - half * s2
+    h0, h1, h2 = 0.5 * s0, 0.5 * s1, 0.5 * s2
+    if sign > 0:
+        t0, t1, t2 = h0 + d1, h1 + d1, h2 - d2
+        base = centre + 0.5 * d1
+    else:
+        t0, t1, t2 = h0 - d1, h1 - d1, h2 + d2
+        base = centre - 0.5 * d1
     r0, r1, r2 = inverse_of(m0 + t0 * t0), inverse_of(m1 + t1 * t1), inverse_of(m2 + t2 * t2)
     w0, w1, w2 = r0 * r0, 6.0 * (r1 * r1), 3.0 * (r2 * r2)
     scale = inverse_of(w0 + w1 + w2)
     w0, w1, w2 = w0 * scale, w1 * scale, w2 * scale
-    e0, e1 = (1.0 / 3.0) * s0, (1.0 / 3.0) * s1
-    e2 = 0.5 * s1 - (1.0 / 6.0) * s2
+    third, sixth = 1.0 / 3.0, 1.0 / 6.0
+    e0, e1, e2 = third * s0, third * s1, h1 - sixth * s2
     mean = w0 * e0 + w1 * e1 + w2 * e2
-    face = centre + half * d1 + mean
-    c0 = w0 * r0 * (mean - e0)
-    c1 = w1 * r1 * (mean - e1)
-    c2 = w2 * r2 * (mean - e2)
-    c0, c1, c2 = c0 + c0, c1 + c1, c2 + c2
-    k = 13.0 / 6.0
-    p0, p1, p2 = c0 * t0, c1 * t1, c2 * t2
-    third = 1.0 / 3.0
-    if sign > 0:
-        a0 = third * w0 + k * (c0 * s0) + p0
-        a1 = third * w1 + 0.5 * w2 + k * (c1 * s1) + p1
-        a2 = k * (c2 * s2) - (1.0 / 6.0) * w2 - p2
-    else:
-        a0 = third * w0 + k * (c0 * s0) - p0
-        a1 = third * w1 + 0.5 * w2 + k * (c1 * s1) - p1
-        a2 = k * (c2 * s2) - (1.0 / 6.0) * w2 + p2
-    g1 = half + 2.0 * (p0 + p1)
-    g2 = 2.0 * p2
-    return face, (a0, a1, a2, g1, g2)
+    c0, c1, c2 = w0 * r0 * (mean - e0), w1 * r1 * (mean - e1), w2 * r2 * (mean - e2)
+    k = 13.0 / 3.0
+    p0, p1, p2 = 2.0 * (c0 * t0), 2.0 * (c1 * t1), 2.0 * (c2 * t2)
+    a0 = third * w0 + k * (c0 * s0) + p0
+    a1 = third * w1 + 0.5 * w2 + k * (c1 * s1) + p1
+    a2 = k * (c2 * s2) - sixth * w2 + p2
+    j1 = a1 - 2.0 * a0 - (0.5 + 2.0 * (p0 + p1))
+    j3 = a1 - 2.0 * (a2 + p2)
+    j2 = 1.0 - (a0 + a2) - (j1 + j3)
+    return base + mean, (a0, j1, j2, j3, a2)
+
+
+def weno_of(v0, v1, v2, v3, v4):
+    d0, d1, d2, d3 = v1 - v0, v2 - v1, v3 - v2, v4 - v3
+    s0, s1, s2 = d1 - d0, d2 - d1, d3 - d2
+    return weno(v2, d1, d2, s0, s1, s2, rough(s0), rough(s1), rough(s2), 1)
 
 
 def ring_weno(f, axis, sign):
-    ahead = shifted(f, 1, axis) - f
-    behind = shifted(ahead, -1, axis)
-    bend = ahead - behind
-    m = rough(bend)
-    below, above = shifted(bend, -1, axis), shifted(bend, 1, axis)
-    if sign > 0:
-        return weno(f, behind, ahead, below, bend, above, rough(below), m, rough(above), 1.0)
-    return weno(f, ahead, behind, above, bend, below, rough(above), m, rough(below), -1.0)
+    v = [shifted(f, k, axis) if k else f for k in (-2, -1, 0, 1, 2)]
+    return weno_of(*v[::sign])
 
 
 def ring_weno_back(mu, coef, axis, sign):
-    a0, a1, a2, g1, g2 = [k * mu for k in coef]
-    if sign > 0:
-        bend = shifted(a0, 1, axis) + a1 + shifted(a2, -1, axis)
-        ahead = g2 + bend + shifted(g1 - bend, 1, axis)
-    else:
-        bend = shifted(a0, -1, axis) + a1 + shifted(a2, 1, axis)
-        ahead = g1 + bend + shifted(g2 - bend, 1, axis)
-    return mu + shifted(ahead, -1, axis) - ahead
+    total = coef[2] * mu
+    for k in (0, 1, 3, 4):
+        total = total + shifted(coef[k] * mu, sign * (2 - k), axis)
+    return total
 
 
 def plus(total, term):
@@ -131,22 +123,64 @@
 
 
 def kernel(
-    n, state, closure, cotangent, out_state, out_closure,
+    n, state, closure_in, cotangent, out_state, out_closure, closure,
     q, other, coef_x, coef_y, coef_z, lap, fx, fy, fz, rate,
     lam, weight, total, gx, go, gin, rx_low, rx_high, ro, send, recv,
+    home, home_closure, grad_closure, route_send, route_recv,
 ):
     wide = n + 2 * HALO
     mine = pl.ds(HALO, n)
     count = lax.axis_size("gx")
     me = lax.axis_index("gx")
-    right, left = lax.rem(me + 1, count), lax.rem(me + count - 1, count)
+    folded = count == 8
+    if folded:
+        block = lax.rem(me // 2 + (me % 2) * (count - 1 - 2 * (me // 2)) + 2, count)
+    else:
+        block = me
+
+    def around(b):
+        return lax.rem(b + 2 * count, count)
+
+    def place(b):
+        if not folded:
+            return around(b)
+        b = around(b - 2)
+        return 2 * b + (b // (count // 2)) * (2 * count - 1 - 4 * b)
+
+    right, left = place(block + 1), place(block - 1)
     across = 1 - lax.axis_index("gy")
     barrier = pltpu.get_barrier_semaphore()
-    for target in ({"gx": left}, {"gx": right}, {"gy": across}):
+    greeted = [{"gx": around(me + k)} for k in (range(1, count) if folded else (1, -1))]
+    for target in greeted + [{"gy": across}]:
         pl.semaphore_signal(barrier, inc=1, device_id=target, device_id_type=MESH)
-
-    q[0, :, mine] = state[...]
-    pl.semaphore_wait(barrier, 3)
+    pl.semaphore_wait(barrier, len(greeted) + 1)
+    leaving = []
+
+    def route(number, source, landing, target, hop):
+        remote = pltpu.make_async_remote_copy(
+            src_ref=source, dst_ref=landing,
+            send_sem=route_send.at[number], recv_sem=route_recv.at[number],
+            device_id={"gx": target}, device_id_type=MESH,
+        )
+        here = pltpu.make_async_copy(source, landing, route_recv.at[number])
+        if folded:
+            pl.when(target == me)(here.start)
+            pl.when(target != me)(remote.start)
+            leaving.append(lambda: pl.when(target != me)(remote.wait_send))
+            return remote.wait_recv
+        if hop == 0:
+            here.start()
+            return here.wait
+        remote.start()
+        leaving.append(remote.wait_send)
+        return remote.wait_recv
+
+    got_state = route(0, state, q.at[0, :, mine], place(me), 0)
+    got_high = route(1, state.at[:, pl.ds(0, HALO)], q.at[0, :, pl.ds(n + HALO, HALO)], place(me - 1), -1)
+    got_low = route(2, state.at[:, pl.ds(n - HALO, HALO)], q.at[0, :, pl.ds(0, HALO)], place(me + 1), 1)
+    got_closure = route(3, closure_in, closure, place(me), 0)
+    got_state()
+    late = []
 
     def three(number, sources, targets):
         made = []
@@ -180,7 +214,9 @@
             (q.at[s, :, pl.ds(HALO, HALO)], q.at[s, :, pl.ds(n, HALO)], q.at[s, :, mine]),
             (q.at[s, :, pl.ds(n + HALO, HALO)], q.at[s, :, pl.ds(0, HALO)], other.at[s]),
         )
-        for copy in (copies[2], copies[0], copies[1]):
+        if s == 0:
+            copies = copies[2:]
+        for copy in copies[::-1]:
             copy.start()
         pending.extend(copies)
 
@@ -196,13 +232,13 @@
                 coef_z[s, c, 0, k] = coef[k]
                 coef_z[s, c, 1, k] = coef_low[k]
             if not last:
-                face = face + shifted(face_low, 1, 2)
-                rate[c] = shifted(face, -1, 2) - face
+                rate[c] = (shifted(face, -1, 2) - shifted(face_low, 1, 2)) + (face_low - face)
             own = q[s, c, mine]
             lap[s, c] = shifted(own, -1, 2) + shifted(own, 1, 2) - 6.0 * own
 
-        each(along_z)
-        copies[2].wait_recv()
+        for c in range(5):
+            along_z(c)
+        copies[-1].wait_recv()
         up, down = split_fluxes([ring_y(s, c) for c in range(5)], 1)
         for c in range(5):
             fy[0, c] = up[c]
@@ -215,14 +251,20 @@
                 coef_y[s, c, 0, k] = coef[k]
                 coef_y[s, c, 1, k] = coef_low[k]
             if not last:
-                face = face + shifted(face_low, 1, 1)
-                rate[c] += (shifted(face, -1, 1) - face)[:, :8]
+                moved = shifted(face, -1, 1) - shifted(face_low, 1, 1)
+                rate[c] += (moved + (face_low - face))[:, :8]
             both = ring_y(s, c)
             lap[s, c] += (shifted(both, -1, 1) + shifted(both, 1, 1))[:, :8]
 
         each(along_y)
-        copies[0].wait_recv()
-        copies[1].wait_recv()
+        if s == 0:
+            got_high()
+            got_low()
+            got_closure()
+            late.append(route(4, cotangent, weight, place(me), 0))
+        else:
+            copies[0].wait_recv()
+            copies[1].wait_recv()
 
         def flux_x(i):
             at = pl.ds(2 * i, 2)
@@ -246,12 +288,12 @@
                         i = face + 2
                         value, coef = weno(
                             f[i], d[i - 1], d[i], bend[i - 1], bend[i], bend[i + 1],
-                            m[i - 1], m[i], m[i + 1], 1.0)
+                            m[i - 1], m[i], m[i + 1], 1)
                     else:
                         i = face + 3
                         value, coef = weno(
                             f[i], d[i], d[i - 1], bend[i + 1], bend[i], bend[i - 1],
-                            m[i + 1], m[i], m[i - 1], -1.0)
+                            m[i + 1], m[i], m[i - 1], -1)
                     faces[face] = plus(faces[face], value)
                     for k in range(5):
                         coef_x[s, c, side, k, face] = coef[k]
@@ -274,40 +316,25 @@
 
         def along_x(c):
             on = jnp.where(c > 0, 1.0, 0.0)
-            load = []
+            lams = []
             for x in range(n):
                 here = weight[c, x]
-                total[c, x] += weight_base * here
-                load.append((TIME_STEP * weight_section) * here)
-                lam[c, x] = load[x]
+                if weight_base:
+                    total[c, x] += weight_base * here
+                lams.append((TIME_STEP * weight_section) * here)
+                lam[c, x] = lams[x]
                 gin[c, x] = weight_section * here
-            mus = [load[0]] + [load[x] - load[x - 1] for x in range(1, n)] + [-load[n - 1]]
+            mus = [lams[0]] + [lams[x] - lams[x - 1] for x in range(1, n)] + [-lams[n - 1]]
             for side, sign in ((0, 1), (1, -1)):
-                bend = [None] * wide
-                ahead = [None] * wide
                 value = [None] * wide
                 for face in range(n + 1):
-                    mu = mus[face]
-                    a0, a1, a2, g1, g2 = [coef_x[s, c, side, k, face] * mu for k in range(5)]
                     i = face + 2 if sign > 0 else face + 3
-                    value[i] = mu
-                    bend[i] = plus(bend[i], a1)
-                    bend[i - sign] = plus(bend[i - sign], a0)
-                    bend[i + sign] = plus(bend[i + sign], a2)
-                    first, second = (i - 1, i) if sign > 0 else (i, i - 1)
-                    ahead[first] = plus(ahead[first], g1)
-                    ahead[second] = plus(ahead[second], g2)
-                for i in range(wide):
-                    if bend[i] is not None:
-                        ahead[i] = plus(ahead[i], bend[i])
-                        ahead[i - 1] = plus(ahead[i - 1], -bend[i])
-                for i in range(wide):
-                    if ahead[i] is not None:
-                        value[i + 1] = plus(value[i + 1], ahead[i])
-                        value[i] = plus(value[i], -ahead[i])
+                    for k in range(5):
+                        at = i + sign * (k - 2)
+                        value[at] = plus(value[at], coef_x[s, c, side, k, face] * mus[face])
                 for i in range(wide):
                     fx[side, c, i] = jnp.zeros_like(mus[0]) if value[i] is None else value[i]
-            kappa = [on * closure[x] * load[x] for x in range(n)]
+            kappa = [on * closure[x] * lams[x] for x in range(n)]
             for i in range(wide):
                 x = i - HALO
                 term = None
@@ -336,8 +363,15 @@
             (gx.at[s, :, pl.ds(0, HALO)], gx.at[s, :, pl.ds(n + HALO, HALO)], go.at[s]),
             (rx_high.at[s], rx_low.at[s], ro.at[s]),
         )
-        copies[0].start()
-        copies[1].start()
+        if s == 0:
+            copies = copies[2:]
+            arrivals.append(route(
+                5, gx.at[s, :, pl.ds(0, HALO)], rx_high.at[s], around(block - 1), -1))
+            arrivals.append(route(
+                6, gx.at[s, :, pl.ds(n + HALO, HALO)], rx_low.at[s], around(block + 1), 1))
+        else:
+            copies[0].start()
+            copies[1].start()
 
         def along_y(c):
             on = jnp.where(c > 0, 1.0, 0.0)
@@ -365,7 +399,7 @@
                 go[s, c, x] += grad[c][8:]
 
         each(pull_y, n)
-        copies[2].start()
+        copies[-1].start()
         pending.extend(copies)
 
         def along_z(c):
@@ -375,7 +409,8 @@
             fz[0, c] = ring_weno_back(mu, [coef_z[s, c, 0, k] for k in range(5)], 2, 1)
             fz[1, c] = ring_weno_back(nu, [coef_z[s, c, 1, k] for k in range(5)], 2, -1)
 
-        each(along_z)
+        for c in range(5):
+            along_z(c)
 
         def pull_z(i):
             at = pl.ds(2 * i, 2)
@@ -391,24 +426,43 @@
         share = lam[1] * lap[s, 1]
         for c in range(2, 5):
             share = share + lam[c] * lap[s, c]
-        out_closure[...] = share if s == 2 else out_closure[...] + share
+        grad_closure[...] = share if s == 2 else grad_closure[...] + share
+        if s == 0:
+            arrivals.append(route(7, grad_closure, home_closure, block, 0))
         for copy in copies:
             copy.wait_recv()
 
         def gather(c):
+            if s == 0:
+                gin[c] = gin[c] + ro[s, c] + total[c]
+                return
             weight[c] = gin[c] + ro[s, c]
             weight[c, pl.ds(n - HALO, HALO)] += rx_high[s, c]
             weight[c, pl.ds(0, HALO)] += rx_low[s, c]
 
         each(gather)
-
+        if s == 0:
+            arrivals.append(route(8, gin, home, block, 0))
+
+    arrivals = []
     for s in range(3):
         forward(s)
-    weight[...] = cotangent[...]
+    late[0]()
     total[...] = jnp.zeros_like(total)
     for s in (2, 1, 0):
         backward(s)
-    out_state[...] = total[...] + weight[...]
+    for arrived in arrivals:
+        arrived()
+    out_closure[...] = home_closure[...]
+
+    def finish(c):
+        out_state[c] = home[c]
+        out_state[c, pl.ds(n - HALO, HALO)] += rx_high[0, c]
+        out_state[c, pl.ds(0, HALO)] += rx_low[0, c]
+
+    each(finish)
+    for wait in leaving:
+        wait()
     for copy in pending:
         copy.wait_send()
 
@@ -431,9 +485,10 @@
             jax.ShapeDtypeStruct(state.shape, f32),
             jax.ShapeDtypeStruct(closure.shape, f32),
         ),
-        in_specs=[pl.BlockSpec(memory_space=pltpu.VMEM)] * 3,
+        in_specs=[pl.BlockSpec(memory_space=pl.ANY)] * 3,
         out_specs=(pl.BlockSpec(memory_space=pltpu.VMEM),) * 2,
         scratch_shapes=[
+            vmem(n),
             vmem(3, 5, wide), vmem(3, 5, n),
             vmem(3, 5, 2, 5, n + 1), tall(3, 5, 2, 5, n), vmem(3, 5, 2, 5, n),
             vmem(3, 5, n), vmem(2, 5, wide), tall(2, 5, n), vmem(2, 5, n), vmem(5, n),
@@ -441,9 +496,11 @@
             vmem(3, 5, wide), vmem(3, 5, n), vmem(5, n),
             vmem(3, 5, HALO), vmem(3, 5, HALO), vmem(3, 5, n),
             pltpu.SemaphoreType.DMA((6, 3)), pltpu.SemaphoreType.DMA((6, 3)),
+            vmem(5, n), vmem(n), vmem(n),
+            pltpu.SemaphoreType.DMA((9,)), pltpu.SemaphoreType.DMA((9,)),
         ],
         compiler_params=pltpu.CompilerParams(
-            collective_id=0, has_side_effects=True, vmem_limit_bytes=40 * 1024 * 1024
+            collective_id=0, has_side_effects=True, vmem_limit_bytes=56 * 1024 * 1024
         ),
     )(state, closure, cotangent)
 

time: 42 us -> 40.3 us (0.960)
  local copies, waits for them, and re-layouts: 3.73 us -> 2.14 us
    unnamed x8 -> x4, local copies, waits for them, and re-layouts: 3.73 us -> 2.14 us
where the time goes in v2:
time: 40.3 us; the launch traced here: 40.1 us
  Pallas kernels  37.3 us (93%)
  local copies, waits for them, and re-layouts  2.14 us (5%)
  between operations  0.65 us (2%)
    pallas_call x1, Pallas kernels, local(): pl.pallas_call(functools.partial(kernel, n), out_shape=(jax.ShapeDtypeStr...  37.3 us
    unnamed x4, local copies, waits for them, and re-layouts  2.14 us

profile of v2, /device:TPU:0, one launch (start us, length us, event | category | flops | bytes accessed | tf_op | source)
XLA Modules:
  0.0 40.1 jit_solution(4633497718532191427)
XLA Ops:
  0.6 37.3 %shard_map.50 = (f32[5,4,8,128]{3,2,1,0:T(8,128)}, f32[4,8,128]{2,1,0:T(8,128)}) custom-call(f32[5,4,8,128]{3,2,1,0:T(8,128)} %state.1, f32[4,8,128]{2,1,0:T(8,128)} %closure_in.1, f32[5,4,8,128]{3,2,1,0:T(8,128)} %cotangent.1), custom_call_target="tpu_custom_call" | custom-call | tf_op jit(solution)/shard_map/pallas_call | solution.py:482
  38.0 0.0 copy-start
  38.0 1.5 %copy.7 = f32[5,4,8,128]{3,2,1,0:T(8,128)} copy(f32[5,4,8,128]{3,2,1,0:T(8,128)} %get-tuple-element.4) | data formatting | bytes 163840
  39.5 0.0 copy-done
  39.5 0.6 %copy.8 = f32[4,8,128]{2,1,0:T(8,128)} copy(f32[4,8,128]{2,1,0:T(8,128)S(1)} %copy-done) | data formatting | bytes 32768
Async XLA Ops:
  38.0 1.5 %copy-start = (f32[4,8,128]{2,1,0:T(8,128)S(1)}, f32[4,8,128]{2,1,0:T(8,128)}, u32[]{:S(2)}) copy-start(f32[4,8,128]{2,1,0:T(8,128)} %get-tuple-element.5) | copy-start | bytes 49156

commit v3 on v2

--- a/solution.py
+++ b/solution.py
@@ -197,6 +197,7 @@
         return made
 
     pending = []
+    deferred = []
 
     def each(body, length=5):
         def step(i, carry):
@@ -219,6 +220,8 @@
         for copy in copies[::-1]:
             copy.start()
         pending.extend(copies)
+        while deferred:
+            each(deferred.pop())
 
         up, down = split_fluxes([q[s, c, mine] for c in range(5)], 2)
         for c in range(5):
@@ -276,7 +279,13 @@
         each(flux_x, wide // 2)
         weight_base, weight_section = SECTION_WEIGHTS[s]
 
-        def along_x(c):
+        def coefs_x(c):
+            along_x(c, False, True)
+
+        def values_x(c):
+            along_x(c, True, last)
+
+        def along_x(c, update, store):
             faces = [None] * (n + 1)
             for side, sign in ((0, 1), (1, -1)):
                 f = [fx[side, c, i] for i in range(wide)]
@@ -296,7 +305,10 @@
                             m[i + 1], m[i], m[i - 1], -1)
                     faces[face] = plus(faces[face], value)
                     for k in range(5):
-                        coef_x[s, c, side, k, face] = coef[k]
+                        if store:
+                            coef_x[s, c, side, k, face] = coef[k]
+            if not update:
+                return
             on = jnp.where(c > 0, 1.0, 0.0)
             for x in range(n):
                 i = x + HALO
@@ -309,7 +321,9 @@
                         weight_base * q[0, c, i] + weight_section * (q[s, c, i] + TIME_STEP * speed)
                     )
 
-        each(along_x)
+        each(values_x)
+        if not last:
+            deferred.append(coefs_x)
 
     def backward(s):
         weight_base, weight_section = SECTION_WEIGHTS[s]
@@ -348,8 +362,8 @@
 
         each(along_x)
 
-        def pull_x(i):
-            at = pl.ds(2 * i, 2)
+        def pull_x(start, width):
+            at = pl.ds(start, width)
             grad = split_fluxes_back(
                 [q[s, c, at] for c in range(5)],
                 [fx[0, c, at] for c in range(5)],
@@ -357,7 +371,8 @@
             for c in range(5):
                 gx[s, c, at] += grad[c]
 
-        each(pull_x, wide // 2)
+        pull_x(0, HALO)
+        pull_x(n + HALO, HALO)
         copies = three(
             HALO + s,
             (gx.at[s, :, pl.ds(0, HALO)], gx.at[s, :, pl.ds(n + HALO, HALO)], go.at[s]),
@@ -372,6 +387,7 @@
         else:
             copies[0].start()
             copies[1].start()
+        pull_x(HALO, n)
 
         def along_y(c):
             on = jnp.where(c > 0, 1.0, 0.0)

time: 40.3 us -> 39.8 us (0.988)
    pallas_call x1, Pallas kernels: 37.3 us -> 36.9 us  [local(): pl.pallas_call(functools.partial(kernel, n), out_shape=(jax.ShapeDtypeStr...]
where the time goes in v3:
time: 39.8 us; the launch traced here: 39.6 us
  Pallas kernels  36.9 us (93%)
  local copies, waits for them, and re-layouts  2.14 us (5%)
  between operations  0.65 us (2%)
    pallas_call x1, Pallas kernels, local(): pl.pallas_call(functools.partial(kernel, n), out_shape=(jax.ShapeDtypeStr...  36.9 us
    unnamed x4, local copies, waits for them, and re-layouts  2.14 us

profile of v3, /device:TPU:0, one launch (start us, length us, event | category | flops | bytes accessed | tf_op | source)
XLA Modules:
  0.0 39.6 jit_solution(5703158462473254554)
XLA Ops:
  0.6 36.9 %shard_map.50 = (f32[5,4,8,128]{3,2,1,0:T(8,128)}, f32[4,8,128]{2,1,0:T(8,128)}) custom-call(f32[5,4,8,128]{3,2,1,0:T(8,128)} %state.1, f32[4,8,128]{2,1,0:T(8,128)} %closure_in.1, f32[5,4,8,128]{3,2,1,0:T(8,128)} %cotangent.1), custom_call_target="tpu_custom_call" | custom-call | tf_op jit(solution)/shard_map/pallas_call | solution.py:498
  37.5 0.0 copy-start
  37.5 1.5 %copy.7 = f32[5,4,8,128]{3,2,1,0:T(8,128)} copy(f32[5,4,8,128]{3,2,1,0:T(8,128)} %get-tuple-element.4) | data formatting | bytes 163840
  39.0 0.0 copy-done
  39.0 0.6 %copy.8 = f32[4,8,128]{2,1,0:T(8,128)} copy(f32[4,8,128]{2,1,0:T(8,128)S(1)} %copy-done) | data formatting | bytes 32768
Async XLA Ops:
  37.5 1.5 %copy-start = (f32[4,8,128]{2,1,0:T(8,128)S(1)}, f32[4,8,128]{2,1,0:T(8,128)}, u32[]{:S(2)}) copy-start(f32[4,8,128]{2,1,0:T(8,128)} %get-tuple-element.5) | copy-start | bytes 49156
